TPU v7x, 512 devices: a whole 4x8x8 slice. The times are simulated.
512 devices in a mesh: pair: 32 (over y, x), row: 16 (over z, core).
Axes of the slice: x: 4, y: 8, z: 8, core: 2. Of those that a mesh axis runs over, the one named last changes fastest.
Arguments:
- activations: float32 [32768, 8192], P('row', 'pair')
- lead: int32 [32], P('pair'), may hold values from 0 to 1
Outputs:
- rotated: float32 [32768, 8192], P('row', 'pair')
All inputs are finite; a program needn't handle non-finite values.
Results may differ from a plain program's by a relative error of at most 0.00075.
Values sent between devices are 32-bit elements; how exact they have to be, the bound alone decides.
A program may use at most 64 MiB of HBM per device.

v0:
```python
import jax
import jax.numpy as jnp
from jax import lax
from jax.sharding import PartitionSpec as P

ROUNDS = 6


epsilon = 1e-06


def passed_along(value, axis, steps):
    count = lax.axis_size(axis)
    initial, last = (max(0, -steps), min(count, count - steps))
    return lax.ppermute(value, axis, [(source, source + steps) for source in range(initial, last)])


def product(left, right):
    return jnp.dot(left, right, precision=lax.Precision.HIGHEST, preferred_element_type=jnp.float32)


def inner_rows(left, right):
    return lax.dot_general(
        left,
        right,
        (((0,), (0,)), ((), ())),
        precision=lax.Precision.HIGHEST,
        preferred_element_type=jnp.float32,
    )


def inverse_of(matrix):
    factor = jnp.linalg.cholesky(matrix)
    identity = jnp.eye(matrix.shape[0], dtype=matrix.dtype)
    return jax.scipy.linalg.cho_solve((factor, True), identity)


def rotation(coupling):
    width = coupling.shape[0]
    identity = jnp.eye(width, dtype=coupling.dtype)
    left_inverse = inverse_of(identity + product(coupling, coupling.T))
    right_inverse = inverse_of(identity + product(coupling.T, coupling))
    lead_column = jnp.concatenate(
        [2.0 * left_inverse - identity, 2.0 * product(coupling.T, left_inverse)], axis=0
    )
    trail_column = jnp.concatenate(
        [-2.0 * product(coupling, right_inverse), 2.0 * right_inverse - identity], axis=0
    )
    return (lead_column, trail_column)


def shards(activations, lead):
    width = activations.shape[1] // 2
    first_block = activations[:, :width]
    second_block = activations[:, width:]
    swapped = lead[0] == 1
    leading = jnp.where(swapped, second_block, first_block)
    trailing = jnp.where(swapped, first_block, second_block)
    position = lax.axis_index("pair")
    seats = lax.axis_size("pair")
    for sweep_round in range(ROUNDS):
        paired = jnp.concatenate([leading, trailing], axis=1)
        gram = lax.psum(inner_rows(paired, paired), "row")
        gram_cross = gram[:width, width:]
        norms = jnp.diagonal(gram)
        norms_lead = norms[:width]
        norms_trail = norms[width:]
        coupling = gram_cross / (norms_lead[:, None] + norms_trail[None, :] + epsilon)
        lead_column, trail_column = rotation(coupling)
        new_lead = product(paired, lead_column)
        new_trail = product(paired, trail_column)
        if sweep_round + 1 < ROUNDS:
            going_up = jnp.where(position == 0, new_trail, new_lead)
            from_below = passed_along(going_up, "pair", 1)
            from_above = passed_along(new_trail, "pair", -1)
            leading = jnp.where(position == 0, new_lead, from_below)
            trailing = jnp.where(position == seats - 1, new_lead, from_above)
        else:
            leading = new_lead
            trailing = new_trail
    return jnp.concatenate([leading, trailing], axis=1)


def solution(mesh):
    return jax.shard_map(
        shards,
        mesh=mesh,
        in_specs=(P("row", "pair"), P("pair")),
        out_specs=P("row", "pair"),
        check_vma=False,
    )
```

profile of v0, /device:TPU:1, one launch (start us, length us, event | category | flops | bytes accessed | tf_op | source)
XLA Modules:
  0.0 1219.3 jit_solution(13229418926247733105)
XLA Ops:
  13.6 119.9 %all-reduce.7.cloned.1.call-done = f32[256,256]{1,0:T(8,128)} async-done(((f32[256,256]{1,0:T(8,128)}), f32[256,256]{1,0:T(8,128)}) %all-reduce.7.cloned.1.call-update) | async-done | bytes 262160 | tf_op jit(solution)/shard_map/psum | solution.py:63
  137.5 11.7 cholesky.194
  161.5 11.7 cholesky.205
  174.6 10.3 custom-call.31
  196.6 20.8 %collective-permute-done = f32[2048,128]{0,1:T(8,128)S(1)} collective-permute-done((f32[2048,128]{0,1:T(8,128)}, f32[2048,128]{0,1:T(8,128)S(1)}, u32[]{:S(2)}, u32[]{:S(2)}) %collective-permute-start) | collective-permute-done | bytes 1048608 | tf_op jit(solution)/shard_map/ppermute | solution.py:15
  225.6 116.7 %all-reduce.9.cloned.1.call-done = f32[256,256]{1,0:T(8,128)} async-done(((f32[256,256]{1,0:T(8,128)}), f32[256,256]{1,0:T(8,128)}) %all-reduce.9.cloned.1.call-update) | async-done | bytes 262160 | tf_op jit(solution)/shard_map/psum | solution.py:63
  346.4 11.7 cholesky.216
  370.4 11.7 cholesky.227
  401.8 20.5 %collective-permute-done.2 = f32[2048,128]{0,1:T(8,128)S(1)} collective-permute-done((f32[2048,128]{0,1:T(8,128)S(1)}, f32[2048,128]{0,1:T(8,128)S(1)}, u32[]{:S(2)}, u32[]{:S(2)}) %collective-permute-start.2) | collective-permute-done | bytes 1048608 | tf_op jit(solution)/shard_map/ppermute | solution.py:15
  429.4 116.1 %all-reduce.11.cloned.1.call-done = f32[256,256]{1,0:T(8,128)} async-done(((f32[256,256]{1,0:T(8,128)}), f32[256,256]{1,0:T(8,128)}) %all-reduce.11.cloned.1.call-update) | async-done | bytes 262160 | tf_op jit(solution)/shard_map/psum | solution.py:63
  549.5 11.7 cholesky.238
  573.5 11.7 cholesky.249
  604.9 20.5 %collective-permute-done.4 = f32[2048,128]{0,1:T(8,128)S(1)} collective-permute-done((f32[2048,128]{0,1:T(8,128)S(1)}, f32[2048,128]{0,1:T(8,128)S(1)}, u32[]{:S(2)}, u32[]{:S(2)}) %collective-permute-start.4) | collective-permute-done | bytes 1048608 | tf_op jit(solution)/shard_map/ppermute | solution.py:15
  632.3 116.3 %all-reduce.13.cloned.1.call-done = f32[256,256]{1,0:T(8,128)} async-done(((f32[256,256]{1,0:T(8,128)}), f32[256,256]{1,0:T(8,128)}) %all-reduce.13.cloned.1.call-update) | async-done | bytes 262160 | tf_op jit(solution)/shard_map/psum | solution.py:63
  752.7 11.7 cholesky.260
  776.6 11.7 cholesky.271
  808.3 20.5 %collective-permute-done.6 = f32[2048,128]{0,1:T(8,128)S(1)} collective-permute-done((f32[2048,128]{0,1:T(8,128)S(1)}, f32[2048,128]{0,1:T(8,128)S(1)}, u32[]{:S(2)}, u32[]{:S(2)}) %collective-permute-start.6) | collective-permute-done | bytes 1048608 | tf_op jit(solution)/shard_map/ppermute | solution.py:15
  835.6 116.3 %all-reduce.15.cloned.1.call-done = f32[256,256]{1,0:T(8,128)} async-done(((f32[256,256]{1,0:T(8,128)}), f32[256,256]{1,0:T(8,128)}) %all-reduce.15.cloned.1.call-update) | async-done | bytes 262160 | tf_op jit(solution)/shard_map/psum | solution.py:63
  956.0 11.7 cholesky.282
  980.0 11.7 cholesky.293
  1011.6 20.5 %collective-permute-done.8 = f32[2048,128]{0,1:T(8,128)S(1)} collective-permute-done((f32[2048,128]{0,1:T(8,128)S(1)}, f32[2048,128]{0,1:T(8,128)S(1)}, u32[]{:S(2)}, u32[]{:S(2)}) %collective-permute-start.8) | collective-permute-done | bytes 1048608 | tf_op jit(solution)/shard_map/ppermute | solution.py:15
  1038.8 116.6 %all-reduce.17.cloned.1.call-done = f32[256,256]{1,0:T(8,128)} async-done(((f32[256,256]{1,0:T(8,128)}), f32[256,256]{1,0:T(8,128)}) %all-reduce.17.cloned.1.call-update) | async-done | bytes 262160 | tf_op jit(solution)/shard_map/psum | solution.py:63
  1159.4 11.7 cholesky.304
  1183.4 11.9 cholesky.315
  (223 shorter events, 248.2 us)
Async XLA Ops:
  6.5 126.9 %all-reduce.7.cloned.1.call-start = ((), (), s32[]{:S(2)}) async-start(), calls=%async_computation | async-start | bytes 524288 | tf_op jit(solution)/shard_map/psum | solution.py:63
  13.2 329.1 %all-reduce.9.cloned.1.call-start = ((), (), s32[]{:S(2)}) async-start(), calls=%async_computation.1 | async-start | bytes 524288 | tf_op jit(solution)/shard_map/psum | solution.py:63
  133.5 27.5 %copy-start = (f32[256,256]{1,0:T(8,128)S(1)}, f32[256,256]{1,0:T(8,128)}, u32[]{:S(2)}) copy-start(f32[256,256]{1,0:T(8,128)} %all-reduce.7.cloned.1.call-done) | copy-start | bytes 786436
  192.1 25.3 %collective-permute-start = (f32[2048,128]{0,1:T(8,128)}, f32[2048,128]{0,1:T(8,128)S(1)}, u32[]{:S(2)}, u32[]{:S(2)}) collective-permute-start(f32[2048,128]{0,1:T(8,128)} %get-tuple-element.31), channel_id=1, source_target_pairs={{0,16},{16,32},{32,48},{48,64},{64,80},{80,96},{96,112},{112,128},... | collective-permute-start | bytes 3145736 | tf_op jit(solution)/shard_map/ppermute | solution.py:15
  195.3 26.0 %collective-permute-start.1 = (f32[2048,128]{0,1:T(8,128)}, f32[2048,128]{0,1:T(8,128)}, u32[]{:S(2)}, u32[]{:S(2)}) collective-permute-start(f32[2048,128]{0,1:T(8,128)} %get-tuple-element.32), channel_id=1, source_target_pairs={{16,0},{32,16},{48,32},{64,48},{80,64},{96,80},{112,96},{128,112},... | collective-permute-start | bytes 3145736 | tf_op jit(solution)/shard_map/ppermute | solution.py:15
  217.4 1.0 copy-start.6
  225.4 320.1 %all-reduce.11.cloned.1.call-start = ((), (), s32[]{:S(2)}) async-start(), calls=%async_computation.2 | async-start | bytes 524288 | tf_op jit(solution)/shard_map/psum | solution.py:63
  342.3 27.5 %copy-start.1 = (f32[256,256]{1,0:T(8,128)S(1)}, f32[256,256]{1,0:T(8,128)}, u32[]{:S(2)}) copy-start(f32[256,256]{1,0:T(8,128)} %all-reduce.9.cloned.1.call-done) | copy-start | bytes 786436
  397.3 25.0 %collective-permute-start.2 = (f32[2048,128]{0,1:T(8,128)S(1)}, f32[2048,128]{0,1:T(8,128)S(1)}, u32[]{:S(2)}, u32[]{:S(2)}) collective-permute-start(f32[2048,128]{0,1:T(8,128)S(1)} %get-tuple-element.33), channel_id=1, source_target_pairs={{0,16},{16,32},{32,48},{48,64},{64,80},{80,96},{96,112},{112,128},... | collective-permute-start | bytes 3145736 | tf_op jit(solution)/shard_map/ppermute | solution.py:15
  400.5 25.6 %collective-permute-start.3 = (f32[2048,128]{0,1:T(8,128)S(1)}, f32[2048,128]{0,1:T(8,128)S(1)}, u32[]{:S(2)}, u32[]{:S(2)}) collective-permute-start(f32[2048,128]{0,1:T(8,128)S(1)} %get-tuple-element.34), channel_id=1, source_target_pairs={{16,0},{32,16},{48,32},{64,48},{80,64},{96,80},{112,96},{128,112},... | collective-permute-start | bytes 3145736 | tf_op jit(solution)/shard_map/ppermute | solution.py:15
  428.9 319.7 %all-reduce.13.cloned.1.call-start = ((), (), s32[]{:S(2)}) async-start(), calls=%async_computation.3 | async-start | bytes 524288 | tf_op jit(solution)/shard_map/psum | solution.py:63
  545.5 27.5 %copy-start.2 = (f32[256,256]{1,0:T(8,128)S(1)}, f32[256,256]{1,0:T(8,128)}, u32[]{:S(2)}) copy-start(f32[256,256]{1,0:T(8,128)} %all-reduce.11.cloned.1.call-done) | copy-start | bytes 786436
  600.4 25.0 %collective-permute-start.4 = (f32[2048,128]{0,1:T(8,128)S(1)}, f32[2048,128]{0,1:T(8,128)S(1)}, u32[]{:S(2)}, u32[]{:S(2)}) collective-permute-start(f32[2048,128]{0,1:T(8,128)S(1)} %get-tuple-element.35), channel_id=1, source_target_pairs={{0,16},{16,32},{32,48},{48,64},{64,80},{80,96},{96,112},{112,128},... | collective-permute-start | bytes 3145736 | tf_op jit(solution)/shard_map/ppermute | solution.py:15
  603.6 25.6 %collective-permute-start.5 = (f32[2048,128]{0,1:T(8,128)S(1)}, f32[2048,128]{0,1:T(8,128)S(1)}, u32[]{:S(2)}, u32[]{:S(2)}) collective-permute-start(f32[2048,128]{0,1:T(8,128)S(1)} %get-tuple-element.36), channel_id=1, source_target_pairs={{16,0},{32,16},{48,32},{64,48},{80,64},{96,80},{112,96},{128,112},... | collective-permute-start | bytes 3145736 | tf_op jit(solution)/shard_map/ppermute | solution.py:15
  632.0 319.9 %all-reduce.15.cloned.1.call-start = ((), (), s32[]{:S(2)}) async-start(), calls=%async_computation.4 | async-start | bytes 524288 | tf_op jit(solution)/shard_map/psum | solution.py:63
  748.6 27.5 %copy-start.3 = (f32[256,256]{1,0:T(8,128)S(1)}, f32[256,256]{1,0:T(8,128)}, u32[]{:S(2)}) copy-start(f32[256,256]{1,0:T(8,128)} %all-reduce.13.cloned.1.call-done) | copy-start | bytes 786436
  803.8 25.0 %collective-permute-start.6 = (f32[2048,128]{0,1:T(8,128)S(1)}, f32[2048,128]{0,1:T(8,128)S(1)}, u32[]{:S(2)}, u32[]{:S(2)}) collective-permute-start(f32[2048,128]{0,1:T(8,128)S(1)} %get-tuple-element.37), channel_id=1, source_target_pairs={{0,16},{16,32},{32,48},{48,64},{64,80},{80,96},{96,112},{112,128},... | collective-permute-start | bytes 3145736 | tf_op jit(solution)/shard_map/ppermute | solution.py:15
  807.0 25.7 %collective-permute-start.7 = (f32[2048,128]{0,1:T(8,128)S(1)}, f32[2048,128]{0,1:T(8,128)S(1)}, u32[]{:S(2)}, u32[]{:S(2)}) collective-permute-start(f32[2048,128]{0,1:T(8,128)S(1)} %get-tuple-element.38), channel_id=1, source_target_pairs={{16,0},{32,16},{48,32},{64,48},{80,64},{96,80},{112,96},{128,112},... | collective-permute-start | bytes 3145736 | tf_op jit(solution)/shard_map/ppermute | solution.py:15
  835.4 319.9 %all-reduce.17.cloned.1.call-start = ((), (), s32[]{:S(2)}) async-start(), calls=%async_computation.5 | async-start | bytes 524288 | tf_op jit(solution)/shard_map/psum | solution.py:63
  952.0 27.5 %copy-start.4 = (f32[256,256]{1,0:T(8,128)S(1)}, f32[256,256]{1,0:T(8,128)}, u32[]{:S(2)}) copy-start(f32[256,256]{1,0:T(8,128)} %all-reduce.15.cloned.1.call-done) | copy-start | bytes 786436
  1007.2 24.9 %collective-permute-start.8 = (f32[2048,128]{0,1:T(8,128)S(1)}, f32[2048,128]{0,1:T(8,128)S(1)}, u32[]{:S(2)}, u32[]{:S(2)}) collective-permute-start(f32[2048,128]{0,1:T(8,128)S(1)} %get-tuple-element.39), channel_id=1, source_target_pairs={{0,16},{16,32},{32,48},{48,64},{64,80},{80,96},{96,112},{112,128},... | collective-permute-start | bytes 3145736 | tf_op jit(solution)/shard_map/ppermute | solution.py:15
  1010.3 25.6 %collective-permute-start.9 = (f32[2048,128]{0,1:T(8,128)S(1)}, f32[2048,128]{0,1:T(8,128)S(1)}, u32[]{:S(2)}, u32[]{:S(2)}) collective-permute-start(f32[2048,128]{0,1:T(8,128)S(1)} %get-tuple-element.40), channel_id=1, source_target_pairs={{16,0},{32,16},{48,32},{64,48},{80,64},{96,80},{112,96},{128,112},... | collective-permute-start | bytes 3145736 | tf_op jit(solution)/shard_map/ppermute | solution.py:15
  1155.3 27.5 %copy-start.5 = (f32[256,256]{1,0:T(8,128)S(1)}, f32[256,256]{1,0:T(8,128)}, u32[]{:S(2)}) copy-start(f32[256,256]{1,0:T(8,128)} %all-reduce.17.cloned.1.call-done) | copy-start | bytes 786436
Sparse Core Ops, SparseCore 0:
  13.3 120.0 all-reduce.6
  225.5 116.7 all-reduce.8
  429.0 116.4 all-reduce.10
  632.2 116.4 all-reduce.12
  835.5 116.4 all-reduce.14
  1038.9 116.4 all-reduce.16
where the time goes:
time: 1220 us
  waiting for transfers between devices  823 us (67%)
  other arithmetic  280 us (23%)
  matrix products  55.8 us (5%)
  starting transfers between devices  23.7 us (2%)
  local copies, waits for them, and re-layouts  20.8 us (2%)
  between operations  15.4 us (1%)
    psum x6, waiting for transfers between devices, shards(): gram = lax.psum(inner_rows(paired, paired), 'row')  702 us
    another operation x36, other arithmetic, inverse_of(): factor = jnp.linalg.cholesky(matrix)  149 us
    another operation x24, other arithmetic, inverse_of(): return jax.scipy.linalg.cho_solve((factor, True), identity)  127 us
    ppermute x10, waiting for transfers between devices, passed_along(): lax.ppermute(value, axis, [(source, source + steps) for source in range(i...  121 us
    dot_general x36, matrix products, product(): jnp.dot(left, right, precision=lax.Precision.HIGHEST, preferred_element_t...  32.7 us
  transfers between devices with their start and end apart: 16, of which 16 were waited for; matrix products, arithmetic and copies ran while one was open for 0% of the time, Pallas kernels for 0%

commit v1 on v0

v1 whole, which is shorter than its diff:
```python
import functools

import jax
import jax.numpy as jnp
from jax import lax
from jax.experimental import pallas as pl
from jax.experimental.pallas import tpu as pltpu
from jax.sharding import PartitionSpec as P

ROUNDS = 6
EPSILON = 1e-06
STEPS = 8
CHUNKS = 8
MESH = pl.DeviceIdType.MESH
F32 = jnp.float32
BF16 = jnp.bfloat16


def dot(left, right, contract=((1,), (0,))):
    return lax.dot_general(
        left,
        right,
        (contract, ((), ())),
        precision=lax.Precision.HIGHEST if left.dtype == F32 else None,
        preferred_element_type=F32,
    )


def halves(value):
    high = value.astype(BF16)
    return high, (value - high.astype(F32)).astype(BF16)


def identity_of(width):
    rows = lax.broadcasted_iota(jnp.int32, (width, width), 0)
    columns = lax.broadcasted_iota(jnp.int32, (width, width), 1)
    return (rows == columns).astype(F32)


def inverses(matrices, bound, identity):
    scale = 2.0 / (1.0 + bound)
    gap = (bound - 1.0) / (bound + 1.0)
    rests = [identity - scale * matrix for matrix in matrices]
    found = [scale * identity for _ in matrices]
    for step in range(STEPS):
        factor = 2.0 / (2.0 - gap * gap)
        for i, rest in enumerate(rests):
            if step == 0:
                found[i] = factor * (scale * (identity + rest))
            else:
                found[i] = factor * (found[i] + dot(found[i], rest))
            if step + 1 < STEPS:
                rests[i] = (1.0 - factor) * identity + factor * dot(rest, rest)
        gap = gap * gap / (2.0 - gap * gap)
    for i, matrix in enumerate(matrices):
        found[i] = found[i] + dot(found[i], identity - dot(matrix, found[i]))
    return found


def rotation(coupling):
    identity = identity_of(coupling.shape[0])
    flipped = coupling.T
    bound = 1.0 + jnp.sum(coupling * coupling, keepdims=True)
    left, right = inverses(
        [identity + dot(coupling, flipped), identity + dot(flipped, coupling)], bound, identity
    )
    return (
        (2.0 * left - identity, -2.0 * dot(coupling, right)),
        (2.0 * dot(flipped, left), 2.0 * right - identity),
    )


def kernel(
    seats, group, lead_ref, act_ref, out_ref, held, stage, gram_out, gram_in, coup_out, coup_in,
    up_send, up_recv, down_send, down_recv, gram_send, gram_recv, coup_send, coup_recv,
):
    rows = act_ref.shape[0]
    width = act_ref.shape[1] // 2
    size = rows // CHUNKS
    band = width // group
    seat = lax.axis_index("pair")
    me = lax.axis_index("row")
    above = lax.rem(seat + 1, seats)
    below = lax.rem(seat + seats - 1, seats)
    swapped = lead_ref[0] == 1

    barrier = pltpu.get_barrier_semaphore()
    for step in range(1, group):
        pl.semaphore_signal(
            barrier, inc=1, device_id={"row": lax.rem(me + step, group)}, device_id_type=MESH
        )
    for condition, other in ((seat > 0, below), (seat < seats - 1, above)):
        @pl.when(condition)
        def _():
            pl.semaphore_signal(barrier, inc=1, device_id={"pair": other}, device_id_type=MESH)
    pl.semaphore_wait(
        barrier, group - 1 + (seat > 0).astype(jnp.int32) + (seat < seats - 1).astype(jnp.int32)
    )

    def part(c):
        return pl.ds(c * size, size)

    def up_copy(slot, c):
        return pltpu.make_async_remote_copy(
            src_ref=stage.at[0, part(c)], dst_ref=held.at[slot, 0, part(c)],
            send_sem=up_send.at[c], recv_sem=up_recv.at[slot, c],
            device_id={"pair": above}, device_id_type=MESH,
        )

    def down_copy(slot, c):
        return pltpu.make_async_remote_copy(
            src_ref=stage.at[1, part(c)], dst_ref=held.at[slot, 1, part(c)],
            send_sem=down_send.at[c], recv_sem=down_recv.at[slot, c],
            device_id={"pair": below}, device_id_type=MESH,
        )

    def gram_part(leading, trailing, totals):
        lead_high, lead_low = halves(leading)
        trail_high, trail_low = halves(trailing)
        both = dot(
            jnp.concatenate([lead_high, lead_low], axis=1),
            jnp.concatenate([trail_high, trail_low], axis=1),
            ((0,), (0,)),
        )
        cross = both[:width, :width] + (both[:width, width:] + both[width:, :width])
        norms = [
            jnp.sum((block * block).reshape(-1, 8, width), axis=0) for block in (leading, trailing)
        ]
        new = (cross, *norms)
        return new if totals is None else tuple(a + b for a, b in zip(totals, new))

    def coupling_of(cross, norm_lead, norm_trail):
        norm_lead = jnp.sum(norm_lead, axis=0, keepdims=True)
        norm_trail = jnp.sum(norm_trail, axis=0, keepdims=True)
        line = lax.broadcasted_iota(jnp.int32, (8, width), 0)
        norms = jnp.where(line == 0, norm_lead, jnp.where(line == 1, norm_trail, 0.0))
        for k in range(group):
            gram_out[k, :band] = cross[k * band : (k + 1) * band]
            gram_out[k, band:] = norms
        for step in range(1, group):
            other = lax.rem(me + step, group)
            pltpu.make_async_remote_copy(
                src_ref=gram_out.at[other], dst_ref=gram_in.at[step],
                send_sem=gram_send, recv_sem=gram_recv,
                device_id={"row": other}, device_id_type=MESH,
            ).start()
        total = gram_out[me]
        everything = pltpu.make_async_remote_copy(
            src_ref=gram_out.at[pl.ds(1, group - 1)], dst_ref=gram_in.at[pl.ds(1, group - 1)],
            send_sem=gram_send, recv_sem=gram_recv,
            device_id={"row": lax.rem(me + 1, group)}, device_id_type=MESH,
        )
        everything.wait_recv()
        for step in range(1, group):
            total = total + gram_in[step]
        lane = lax.broadcasted_iota(jnp.int32, (band, width), 1)
        own = lane == me * band + lax.broadcasted_iota(jnp.int32, (band, width), 0)
        column = jnp.sum(jnp.where(own, total[band : band + 1], 0.0), axis=1, keepdims=True)
        coup_out[...] = total[:band] / (column + total[band + 1 : band + 2] + EPSILON)
        for step in range(1, group):
            pltpu.make_async_remote_copy(
                src_ref=coup_out, dst_ref=coup_in.at[step],
                send_sem=coup_send, recv_sem=coup_recv,
                device_id={"row": lax.rem(me + step, group)}, device_id_type=MESH,
            ).start()
        coup_in[0] = coup_out[...]
        arrived = pltpu.make_async_remote_copy(
            src_ref=coup_in.at[pl.ds(1, group - 1)], dst_ref=coup_in.at[pl.ds(1, group - 1)],
            send_sem=coup_send, recv_sem=coup_recv,
            device_id={"row": lax.rem(me + 1, group)}, device_id_type=MESH,
        )
        arrived.wait_recv()
        coupling = jnp.concatenate(
            [coup_in[lax.rem(me - k + group, group)] for k in range(group)], axis=0
        )
        everything.wait_send()
        arrived.wait_send()
        return coupling

    def turn(coupling, swap_rows, swap_columns):
        (lead_lead, lead_trail), (trail_lead, trail_trail) = rotation(coupling)
        top = jnp.concatenate([lead_lead, lead_trail], axis=1)
        bottom = jnp.concatenate([trail_lead, trail_trail], axis=1)
        if swap_rows:
            top, bottom = jnp.where(swapped, bottom, top), jnp.where(swapped, top, bottom)
        whole = jnp.concatenate([top, bottom], axis=0)
        if swap_columns:
            turned = jnp.concatenate([whole[:, width:], whole[:, :width]], axis=1)
            whole = jnp.where(seat == 0, turned, whole)
        return halves(whole)

    def applied(block, turn_high, turn_low):
        high, low = halves(block)
        return dot(high, turn_high) + (dot(high, turn_low) + dot(low, turn_high))

    def apply_and_move(read, turned, slot):
        for c in range(CHUNKS):
            new = applied(read(c), *turned)
            stage[0, part(c)] = new[:, :width]
            stage[1, part(c)] = new[:, width:]

            @pl.when(seat < seats - 1)
            def _():
                up_copy(slot, c).start()

            @pl.when(seat == seats - 1)
            def _():
                held[slot, 1, part(c)] = new[:, :width]

            @pl.when(seat > 0)
            def _():
                down_copy(slot, c).start()

            @pl.when(seat == 0)
            def _():
                held[slot, 0, part(c)] = new[:, width:]

    def arrive(slot, c):
        @pl.when(seat > 0)
        def _():
            up_copy(slot, c).wait_recv()
            down_copy(slot, c).wait_send()

        @pl.when(seat < seats - 1)
        def _():
            down_copy(slot, c).wait_recv()
            up_copy(slot, c).wait_send()

    def moved_coupling(slot):
        totals = None
        for c in range(CHUNKS):
            arrive(slot, c)
            totals = gram_part(held[slot, 0, part(c)], held[slot, 1, part(c)], totals)
        return coupling_of(*totals)

    def held_block(slot, c):
        return jnp.concatenate([held[slot, 0, part(c)], held[slot, 1, part(c)]], axis=1)

    totals = None
    for c in range(CHUNKS):
        totals = gram_part(act_ref[part(c), :width], act_ref[part(c), width:], totals)
    cross, norm_first, norm_second = totals
    coupling = coupling_of(
        jnp.where(swapped, cross.T, cross),
        jnp.where(swapped, norm_second, norm_first),
        jnp.where(swapped, norm_first, norm_second),
    )
    apply_and_move(lambda c: act_ref[part(c)], turn(coupling, True, True), 0)

    def one_round(index, _):
        now = lax.rem(index - 1, 2)
        later = lax.rem(index, 2)
        coupling = moved_coupling(now)
        apply_and_move(lambda c: held_block(now, c), turn(coupling, False, True), later)
        return 0

    lax.fori_loop(1, ROUNDS - 1, one_round, 0)
    last = (ROUNDS - 2) % 2
    turned = turn(moved_coupling(last), False, False)
    for c in range(CHUNKS):
        out_ref[part(c)] = applied(held_block(last, c), *turned)


def shards(activations, lead):
    seats, group = lax.axis_size("pair"), lax.axis_size("row")
    rows, columns = activations.shape
    width = columns // 2
    band = width // group
    dma = pltpu.SemaphoreType.DMA
    return pl.pallas_call(
        functools.partial(kernel, seats, group),
        out_shape=jax.ShapeDtypeStruct((rows, columns), F32),
        in_specs=[
            pl.BlockSpec(memory_space=pltpu.SMEM),
            pl.BlockSpec(memory_space=pltpu.VMEM),
        ],
        out_specs=pl.BlockSpec(memory_space=pltpu.VMEM),
        scratch_shapes=[
            pltpu.VMEM((2, 2, rows, width), F32),
            pltpu.VMEM((2, rows, width), F32),
            pltpu.VMEM((group, band + 8, width), F32),
            pltpu.VMEM((group, band + 8, width), F32),
            pltpu.VMEM((band, width), F32),
            pltpu.VMEM((group, band, width), F32),
            dma((CHUNKS,)),
            dma((2, CHUNKS)),
            dma((CHUNKS,)),
            dma((2, CHUNKS)),
            dma,
            dma,
            dma,
            dma,
        ],
        compiler_params=pltpu.CompilerParams(
            collective_id=0, has_side_effects=True, vmem_limit_bytes=40 * 1024 * 1024
        ),
        cost_estimate=pl.CostEstimate(
            flops=ROUNDS * 2 * rows * columns * (columns + width),
            bytes_accessed=2 * rows * columns * 4,
            transcendentals=0,
        ),
    )(lead, activations)


def solution(mesh):
    return jax.shard_map(
        shards,
        mesh=mesh,
        in_specs=(P("row", "pair"), P("pair")),
        out_specs=P("row", "pair"),
        check_vma=False,
    )
```

time: 1220 us -> 236 us (0.19)
  the two profiles are of different devices: /device:TPU:1 before, /device:TPU:31 now
where the time goes in v1:
time: 236 us
  Pallas kernels  233 us (99%)
  local copies, waits for them, and re-layouts  2.91 us (1%)
    pallas_call x1, Pallas kernels, shards(): pl.pallas_call(functools.partial(kernel, seats, group), out_shape=jax.Sha...  233 us

profile of v1, /device:TPU:31, one launch (start us, length us, event | category | flops | bytes accessed | tf_op | source)
XLA Modules:
  0.0 236.2 jit_solution(9914932135860724425)
XLA Ops:
  0.7 0.0 copy-start
  0.7 1.6 copy-done
  2.2 232.6 %shard_map.28 = f32[2048,256]{1,0:T(8,128)S(1)} custom-call(s32[1]{0:T(128)S(6)} %copy.4.lead_ref, f32[2048,256]{1,0:T(8,128)S(1)} %copy-done), custom_call_target="tpu_custom_call" | custom-call | flops 2415919104 | bytes 4194304 | tf_op jit(solution)/shard_map/pallas_call | solution.py:270
  234.9 1.3 copy.5
Async XLA Ops:
  0.7 1.6 copy-start

commit v2 on v1

v2 whole, which is shorter than its diff:
```python
import functools

import jax
import jax.numpy as jnp
from jax import lax
from jax.experimental import pallas as pl
from jax.experimental.pallas import tpu as pltpu
from jax.sharding import PartitionSpec as P

ROUNDS = 6
EPSILON = 1e-06
STEPS = 8
CHUNKS = 8
MESH = pl.DeviceIdType.MESH
F32 = jnp.float32
BF16 = jnp.bfloat16


def dot(left, right, contract=((1,), (0,))):
    return lax.dot_general(
        left,
        right,
        (contract, ((), ())),
        precision=lax.Precision.HIGHEST if left.dtype == F32 else None,
        preferred_element_type=F32,
    )


def halves(value):
    high = value.astype(BF16)
    return high, (value - high.astype(F32)).astype(BF16)


def identity_of(width):
    rows = lax.broadcasted_iota(jnp.int32, (width, width), 0)
    columns = lax.broadcasted_iota(jnp.int32, (width, width), 1)
    return (rows == columns).astype(F32)


def inverses(matrices, bounds, identity):
    scales = [2.0 / (1.0 + bound) for bound in bounds]
    gaps = [(bound - 1.0) / (bound + 1.0) for bound in bounds]
    rests = [identity - scale * matrix for scale, matrix in zip(scales, matrices)]
    found = [scale * identity for scale in scales]
    for step in range(STEPS):
        for i, rest in enumerate(rests):
            factor = 2.0 / (2.0 - gaps[i] * gaps[i])
            if step == 0:
                found[i] = factor * (scales[i] * (identity + rest))
            else:
                found[i] = factor * (found[i] + dot(found[i], rest))
            if step + 1 < STEPS:
                rests[i] = (1.0 - factor) * identity + factor * dot(rest, rest)
            gaps[i] = gaps[i] * gaps[i] / (2.0 - gaps[i] * gaps[i])
    for i, matrix in enumerate(matrices):
        found[i] = found[i] + dot(found[i], identity - dot(matrix, found[i]))
    return found


def columns_of(lead_coupling, trail_coupling):
    identity = identity_of(lead_coupling.shape[0])
    lead_flipped, trail_flipped = lead_coupling.T, trail_coupling.T
    bounds = [
        1.0 + jnp.sum(coupling * coupling, keepdims=True)
        for coupling in (lead_coupling, trail_coupling)
    ]
    left, right = inverses(
        [
            identity + dot(lead_coupling, lead_flipped),
            identity + dot(trail_flipped, trail_coupling),
        ],
        bounds,
        identity,
    )
    return (
        (2.0 * left - identity, 2.0 * dot(lead_flipped, left)),
        (-2.0 * dot(trail_coupling, right), 2.0 * right - identity),
    )


def kernel(
    seats, group, lead_ref, act_ref, out_ref, held, raw, own, gram_out, gram_in, coup_out, coup_in,
    coup_own, coup_near, turn_own, up_send, up_recv, down_send, down_recv, raw_up_send, raw_up_recv,
    raw_down_send, raw_down_recv, near_up_send, near_up_recv, near_down_send, near_down_recv,
    gram_send, gram_recv, coup_send, coup_recv,
):
    rows = act_ref.shape[0]
    width = act_ref.shape[1] // 2
    size = rows // CHUNKS
    band = width // group
    seat = lax.axis_index("pair")
    me = lax.axis_index("row")
    above = lax.rem(seat + 1, seats)
    below = lax.rem(seat + seats - 1, seats)
    first, final = seat == 0, seat == seats - 1
    swapped = lead_ref[0] == 1

    barrier = pltpu.get_barrier_semaphore()
    for step in range(1, group):
        pl.semaphore_signal(
            barrier, inc=1, device_id={"row": lax.rem(me + step, group)}, device_id_type=MESH
        )
    for condition, other in ((seat > 0, below), (seat < seats - 1, above)):
        @pl.when(condition)
        def _():
            pl.semaphore_signal(barrier, inc=1, device_id={"pair": other}, device_id_type=MESH)
    pl.semaphore_wait(
        barrier, group - 1 + (seat > 0).astype(jnp.int32) + (seat < seats - 1).astype(jnp.int32)
    )

    def part(c):
        return pl.ds(c * size, size)

    def to(other, source, target, send, receive):
        return pltpu.make_async_remote_copy(
            src_ref=source, dst_ref=target, send_sem=send, recv_sem=receive,
            device_id={"pair": other}, device_id_type=MESH,
        )

    def up_copy(c):
        return to(above, own.at[0, 0, part(c)], held.at[0, 0, part(c)], up_send.at[c], up_recv.at[c])

    def down_copy(c):
        return to(
            below, own.at[0, 1, part(c)], held.at[0, 1, part(c)], down_send.at[c], down_recv.at[c]
        )

    def raw_up(slot, c):
        return to(
            above, held.at[slot, 0, part(c)], raw.at[slot, 0, part(c)],
            raw_up_send.at[c], raw_up_recv.at[slot, c],
        )

    def raw_down(slot, c):
        return to(
            below, held.at[slot, 1, part(c)], raw.at[slot, 1, part(c)],
            raw_down_send.at[c], raw_down_recv.at[slot, c],
        )

    def near_up(slot):
        return to(above, coup_own.at[slot], coup_near.at[slot, 0], near_up_send, near_up_recv.at[slot])

    def near_down(slot):
        return to(
            below, coup_own.at[slot], coup_near.at[slot, 1], near_down_send, near_down_recv.at[slot]
        )

    def gram_part(leading, trailing, totals):
        lead_high, lead_low = halves(leading)
        trail_high, trail_low = halves(trailing)
        both = dot(
            jnp.concatenate([lead_high, lead_low], axis=1),
            jnp.concatenate([trail_high, trail_low], axis=1),
            ((0,), (0,)),
        )
        cross = both[:width, :width] + (both[:width, width:] + both[width:, :width])
        norms = [
            jnp.sum((block * block).reshape(-1, 8, width), axis=0) for block in (leading, trailing)
        ]
        new = (cross, *norms)
        return new if totals is None else tuple(a + b for a, b in zip(totals, new))

    gram_all = pltpu.make_async_remote_copy(
        src_ref=gram_out.at[pl.ds(1, group - 1)], dst_ref=gram_in.at[pl.ds(1, group - 1)],
        send_sem=gram_send, recv_sem=gram_recv,
        device_id={"row": lax.rem(me + 1, group)}, device_id_type=MESH,
    )
    coup_all = pltpu.make_async_remote_copy(
        src_ref=coup_in.at[pl.ds(1, group - 1)], dst_ref=coup_in.at[pl.ds(1, group - 1)],
        send_sem=coup_send, recv_sem=coup_recv,
        device_id={"row": lax.rem(me + 1, group)}, device_id_type=MESH,
    )

    def sum_start(cross, norm_lead, norm_trail):
        norm_lead = jnp.sum(norm_lead, axis=0, keepdims=True)
        norm_trail = jnp.sum(norm_trail, axis=0, keepdims=True)
        line = lax.broadcasted_iota(jnp.int32, (8, width), 0)
        norms = jnp.where(line == 0, norm_lead, jnp.where(line == 1, norm_trail, 0.0))
        for k in range(group):
            gram_out[k, :band] = cross[k * band : (k + 1) * band]
            gram_out[k, band:] = norms
        for step in range(1, group):
            other = lax.rem(me + step, group)
            pltpu.make_async_remote_copy(
                src_ref=gram_out.at[other], dst_ref=gram_in.at[step],
                send_sem=gram_send, recv_sem=gram_recv,
                device_id={"row": other}, device_id_type=MESH,
            ).start()

    def sum_end():
        total = gram_out[me]
        gram_all.wait_recv()
        for step in range(1, group):
            total = total + gram_in[step]
        lane = lax.broadcasted_iota(jnp.int32, (band, width), 1)
        mine = lane == me * band + lax.broadcasted_iota(jnp.int32, (band, width), 0)
        column = jnp.sum(jnp.where(mine, total[band : band + 1], 0.0), axis=1, keepdims=True)
        coup_out[...] = total[:band] / (column + total[band + 1 : band + 2] + EPSILON)
        for step in range(1, group):
            pltpu.make_async_remote_copy(
                src_ref=coup_out, dst_ref=coup_in.at[step],
                send_sem=coup_send, recv_sem=coup_recv,
                device_id={"row": lax.rem(me + step, group)}, device_id_type=MESH,
            ).start()
        coup_in[0] = coup_out[...]
        coup_all.wait_recv()
        coupling = jnp.concatenate(
            [coup_in[lax.rem(me - k + group, group)] for k in range(group)], axis=0
        )
        gram_all.wait_send()
        coup_all.wait_send()
        return coupling

    def turn(coupling, swap_rows, swap_columns):
        lead_columns, trail_columns = columns_of(coupling, coupling)
        top, bottom = (
            jnp.concatenate(pair, axis=1) for pair in zip(lead_columns, trail_columns)
        )
        if swap_rows:
            top, bottom = jnp.where(swapped, bottom, top), jnp.where(swapped, top, bottom)
        whole = jnp.concatenate([top, bottom], axis=0)
        if swap_columns:
            turned = jnp.concatenate([whole[:, width:], whole[:, :width]], axis=1)
            whole = jnp.where(first, turned, whole)
        return halves(whole)

    def applied(block, turn_high, turn_low):
        high, low = halves(block)
        return dot(high, turn_high) + (dot(high, turn_low) + dot(low, turn_high))

    def applied_half(block, turn_both):
        high, low = halves(block)
        both = dot(high, turn_both)
        return both[:, :width] + (both[:, width:] + dot(low, turn_both[:, :width]))

    def held_block(slot, c):
        return jnp.concatenate([held[slot, 0, part(c)], held[slot, 1, part(c)]], axis=1)

    totals = None
    for c in range(CHUNKS):
        totals = gram_part(act_ref[part(c), :width], act_ref[part(c), width:], totals)
    cross, norm_first, norm_second = totals
    sum_start(
        jnp.where(swapped, cross.T, cross),
        jnp.where(swapped, norm_second, norm_first),
        jnp.where(swapped, norm_first, norm_second),
    )
    turned = turn(sum_end(), True, True)
    for c in range(CHUNKS):
        new = applied(act_ref[part(c)], *turned)
        own[0, 0, part(c)] = new[:, :width]
        own[0, 1, part(c)] = new[:, width:]

        @pl.when(seat < seats - 1)
        def _():
            up_copy(c).start()

        @pl.when(seat > 0)
        def _():
            down_copy(c).start()

        @pl.when(final)
        def _():
            held[0, 1, part(c)] = new[:, :width]

        @pl.when(first)
        def _():
            held[0, 0, part(c)] = new[:, width:]

    totals = None
    for c in range(CHUNKS):
        @pl.when(seat > 0)
        def _():
            up_copy(c).wait_recv()
            down_copy(c).wait_send()

        @pl.when(seat < seats - 1)
        def _():
            down_copy(c).wait_recv()
            up_copy(c).wait_send()

        leading, trailing = held[0, 0, part(c)], held[0, 1, part(c)]
        totals = gram_part(leading, trailing, totals)

        @pl.when(first)
        def _():
            raw[0, 0, part(c)] = leading
            own[0, 1, part(c)] = trailing

        @pl.when(final)
        def _():
            raw[0, 1, part(c)] = trailing
            own[0, 0, part(c)] = leading

    def forward(slot, c):
        @pl.when(seat < seats - 1)
        def _():
            raw_up(slot, c).start()

        @pl.when(seat > 0)
        def _():
            raw_down(slot, c).start()

    def one_round(index, totals):
        now = lax.rem(index, 2)
        later = 1 - now
        sum_start(*totals)

        @pl.when(index == 2)
        def _():
            for c in range(CHUNKS):
                forward(now, c)

        @pl.when(index > 2)
        def _():
            for c in range(CHUNKS):
                new = applied(held_block(later, c), turn_own[0], turn_own[1])
                own[now, 0, part(c)] = jnp.where(final, held[now, 0, part(c)], new[:, :width])
                own[now, 1, part(c)] = jnp.where(first, held[now, 1, part(c)], new[:, width:])

        coupling = sum_end()
        coup_own[now] = coupling

        @pl.when(seat < seats - 1)
        def _():
            near_up(now).start()

        @pl.when(seat > 0)
        def _():
            near_down(now).start()

        @pl.when(first)
        def _():
            coup_near[now, 0] = coupling

        @pl.when(final)
        def _():
            coup_near[now, 1] = coupling

        turn_own[0], turn_own[1] = turn(coupling, False, True)

        @pl.when(seat > 0)
        def _():
            near_up(now).wait_recv()
            near_down(now).wait_send()

        @pl.when(seat < seats - 1)
        def _():
            near_down(now).wait_recv()
            near_up(now).wait_send()

        low, high = coup_near[now, 0], coup_near[now, 1]
        (low_top, low_bottom), (high_top, high_bottom) = columns_of(
            jnp.where(seat == 1, -low.T, low), jnp.where(final, -high.T, high)
        )
        lead_turn = jnp.concatenate(
            [jnp.where(seat == 1, low_bottom, low_top), jnp.where(seat == 1, low_top, low_bottom)]
        )
        trail_turn = jnp.concatenate(
            [jnp.where(final, high_bottom, high_top), jnp.where(final, high_top, high_bottom)]
        )
        lead_turn = jnp.concatenate(halves(lead_turn), axis=1)
        trail_turn = jnp.concatenate(halves(trail_turn), axis=1)
        totals = None
        for c in range(CHUNKS):
            @pl.when(seat > 0)
            def _():
                raw_up(now, c).wait_recv()
                raw_down(now, c).wait_send()

            @pl.when(seat < seats - 1)
            def _():
                raw_down(now, c).wait_recv()
                raw_up(now, c).wait_send()

            leading = applied_half(
                jnp.concatenate([raw[now, 0, part(c)], own[now, 1, part(c)]], axis=1), lead_turn
            )
            trailing = applied_half(
                jnp.concatenate([own[now, 0, part(c)], raw[now, 1, part(c)]], axis=1), trail_turn
            )
            held[later, 0, part(c)] = leading
            held[later, 1, part(c)] = trailing

            @pl.when(index < ROUNDS - 1)
            def _():
                forward(later, c)

            @pl.when(first)
            def _():
                raw[later, 0, part(c)] = leading

            @pl.when(final)
            def _():
                raw[later, 1, part(c)] = trailing

            totals = gram_part(leading, trailing, totals)
        return totals

    totals = lax.fori_loop(2, ROUNDS, one_round, totals)
    last = ROUNDS % 2
    sum_start(*totals)
    turned = turn(sum_end(), False, False)
    for c in range(CHUNKS):
        out_ref[part(c)] = applied(held_block(last, c), *turned)


def shards(activations, lead):
    seats, group = lax.axis_size("pair"), lax.axis_size("row")
    rows, columns = activations.shape
    width = columns // 2
    band = width // group
    dma = pltpu.SemaphoreType.DMA
    return pl.pallas_call(
        functools.partial(kernel, seats, group),
        out_shape=jax.ShapeDtypeStruct((rows, columns), F32),
        in_specs=[
            pl.BlockSpec(memory_space=pltpu.SMEM),
            pl.BlockSpec(memory_space=pltpu.VMEM),
        ],
        out_specs=pl.BlockSpec(memory_space=pltpu.VMEM),
        scratch_shapes=[
            pltpu.VMEM((2, 2, rows, width), F32),
            pltpu.VMEM((2, 2, rows, width), F32),
            pltpu.VMEM((2, 2, rows, width), F32),
            pltpu.VMEM((group, band + 8, width), F32),
            pltpu.VMEM((group, band + 8, width), F32),
            pltpu.VMEM((band, width), F32),
            pltpu.VMEM((group, band, width), F32),
            pltpu.VMEM((2, width, width), F32),
            pltpu.VMEM((2, 2, width, width), F32),
            pltpu.VMEM((2, columns, columns), BF16),
            dma((CHUNKS,)),
            dma((CHUNKS,)),
            dma((CHUNKS,)),
            dma((CHUNKS,)),
            dma((CHUNKS,)),
            dma((2, CHUNKS)),
            dma((CHUNKS,)),
            dma((2, CHUNKS)),
            dma,
            dma((2,)),
            dma,
            dma((2,)),
            dma,
            dma,
            dma,
            dma,
        ],
        compiler_params=pltpu.CompilerParams(
            collective_id=0, has_side_effects=True, vmem_limit_bytes=48 * 1024 * 1024
        ),
        cost_estimate=pl.CostEstimate(
            flops=ROUNDS * 2 * rows * columns * (2 * columns + width),
            bytes_accessed=2 * rows * columns * 4,
            transcendentals=0,
        ),
    )(lead, activations)


def solution(mesh):
    return jax.shard_map(
        shards,
        mesh=mesh,
        in_specs=(P("row", "pair"), P("pair")),
        out_specs=P("row", "pair"),
        check_vma=False,
    )
```

time: 236 us -> 194 us (0.82)
  Pallas kernels: 233 us -> 191 us
    pallas_call x1, Pallas kernels: 233 us -> 191 us  [shards(): pl.pallas_call(functools.partial(kernel, seats, group), out_shape=jax.Sha...]
where the time goes in v2:
time: 194 us
  Pallas kernels  191 us (98%)
  local copies, waits for them, and re-layouts  2.91 us (2%)
    pallas_call x1, Pallas kernels, shards(): pl.pallas_call(functools.partial(kernel, seats, group), out_shape=jax.Sha...  191 us

profile of v2, /device:TPU:31, one launch (start us, length us, event | category | flops | bytes accessed | tf_op | source)
XLA Modules:
  0.0 194.2 jit_solution(4213892564559536091)
XLA Ops:
  0.7 0.0 copy-start
  0.7 1.6 copy-done
  2.2 190.7 %shard_map.28 = f32[2048,256]{1,0:T(8,128)S(1)} custom-call(s32[1]{0:T(128)S(6)} %copy.4.lead_ref, f32[2048,256]{1,0:T(8,128)S(1)} %copy-done), custom_call_target="tpu_custom_call" | custom-call | flops 4026531840 | bytes 4194304 | tf_op jit(solution)/shard_map/pallas_call | solution.py:414
  192.9 1.3 copy.5
Async XLA Ops:
  0.7 1.6 copy-start

commit v3 on v2

--- a/solution.py
+++ b/solution.py
@@ -11,6 +11,8 @@
 EPSILON = 1e-06
 STEPS = 8
 CHUNKS = 8
+EARLY = 4
+AHEAD = 3
 MESH = pl.DeviceIdType.MESH
 F32 = jnp.float32
 BF16 = jnp.bfloat16
@@ -80,8 +82,9 @@
 
 def kernel(
     seats, group, lead_ref, act_ref, out_ref, held, raw, own, gram_out, gram_in, coup_out, coup_in,
-    coup_own, coup_near, turn_own, up_send, up_recv, down_send, down_recv, raw_up_send, raw_up_recv,
-    raw_down_send, raw_down_recv, near_up_send, near_up_recv, near_down_send, near_down_recv,
+    coup_own, coup_near, up_send, up_recv, down_send, down_recv, raw_up_send, raw_up_recv,
+    raw_down_send, raw_down_recv, ahead_up_send, ahead_up_recv, ahead_down_send, ahead_down_recv,
+    near_up_send, near_up_recv, near_down_send, near_down_recv,
     gram_send, gram_recv, coup_send, coup_recv,
 ):
     rows = act_ref.shape[0]
@@ -103,10 +106,14 @@
     for condition, other in ((seat > 0, below), (seat < seats - 1, above)):
         @pl.when(condition)
         def _():
-            pl.semaphore_signal(barrier, inc=1, device_id={"pair": other}, device_id_type=MESH)
-    pl.semaphore_wait(
-        barrier, group - 1 + (seat > 0).astype(jnp.int32) + (seat < seats - 1).astype(jnp.int32)
-    )
+            for step in range(group):
+                pl.semaphore_signal(
+                    barrier, inc=1, device_id={"pair": other, "row": lax.rem(me + step, group)},
+                    device_id_type=MESH,
+                )
+    beside = (seat > 0).astype(jnp.int32) + (seat < seats - 1).astype(jnp.int32)
+    pl.semaphore_wait(barrier, group - 1 + group * beside)
+    far_first = sorted(range(group), key=lambda step: abs(2 * step - group))
 
     def part(c):
         return pl.ds(c * size, size)
@@ -137,13 +144,26 @@
             raw_down_send.at[c], raw_down_recv.at[slot, c],
         )
 
-    def near_up(slot):
-        return to(above, coup_own.at[slot], coup_near.at[slot, 0], near_up_send, near_up_recv.at[slot])
-
-    def near_down(slot):
+    def ahead_up(c):
         return to(
-            below, coup_own.at[slot], coup_near.at[slot, 1], near_down_send, near_down_recv.at[slot]
-        )
+            above, held.at[1, 1, part(c)], own.at[1, 1, part(c)], ahead_up_send.at[c], ahead_up_recv.at[c]
+        )
+
+    def ahead_down(c):
+        return to(
+            below, held.at[1, 0, part(c)], own.at[1, 0, part(c)],
+            ahead_down_send.at[c], ahead_down_recv.at[c],
+        )
+
+    def near(other, side, slot, step, send, receive):
+        return pltpu.make_async_remote_copy(
+            src_ref=coup_out, dst_ref=coup_near.at[slot, side, step],
+            send_sem=send, recv_sem=receive.at[slot],
+            device_id={"pair": other, "row": lax.rem(me + step, group)}, device_id_type=MESH,
+        )
+
+    def near_all(other, side, slot, send, receive):
+        return to(other, coup_near.at[slot, side], coup_near.at[slot, side], send, receive.at[slot])
 
     def gram_part(leading, trailing, totals):
         lead_high, lead_low = halves(leading)
@@ -160,8 +180,9 @@
         new = (cross, *norms)
         return new if totals is None else tuple(a + b for a, b in zip(totals, new))
 
+    sent = pl.ds(0, band + 2)
     gram_all = pltpu.make_async_remote_copy(
-        src_ref=gram_out.at[pl.ds(1, group - 1)], dst_ref=gram_in.at[pl.ds(1, group - 1)],
+        src_ref=gram_out.at[pl.ds(1, group - 1), sent], dst_ref=gram_in.at[pl.ds(1, group - 1), sent],
         send_sem=gram_send, recv_sem=gram_recv,
         device_id={"row": lax.rem(me + 1, group)}, device_id_type=MESH,
     )
@@ -179,37 +200,56 @@
         for k in range(group):
             gram_out[k, :band] = cross[k * band : (k + 1) * band]
             gram_out[k, band:] = norms
-        for step in range(1, group):
+        for step in far_first[:-1]:
             other = lax.rem(me + step, group)
             pltpu.make_async_remote_copy(
-                src_ref=gram_out.at[other], dst_ref=gram_in.at[step],
+                src_ref=gram_out.at[other, sent], dst_ref=gram_in.at[step, sent],
                 send_sem=gram_send, recv_sem=gram_recv,
                 device_id={"row": other}, device_id_type=MESH,
             ).start()
 
-    def sum_end():
-        total = gram_out[me]
+    def assembled(bands):
+        return jnp.concatenate([bands[lax.rem(me - k + group, group)] for k in range(group)], axis=0)
+
+    def sum_end(slot=None, late=False):
+        total = gram_out[me, :band]
+        norms = gram_out[me, band : band + 2]
         gram_all.wait_recv()
         for step in range(1, group):
-            total = total + gram_in[step]
+            total = total + gram_in[step, :band]
+            norms = norms + gram_in[step, band : band + 2]
         lane = lax.broadcasted_iota(jnp.int32, (band, width), 1)
         mine = lane == me * band + lax.broadcasted_iota(jnp.int32, (band, width), 0)
-        column = jnp.sum(jnp.where(mine, total[band : band + 1], 0.0), axis=1, keepdims=True)
-        coup_out[...] = total[:band] / (column + total[band + 1 : band + 2] + EPSILON)
-        for step in range(1, group):
+        column = jnp.sum(jnp.where(mine, norms[:1], 0.0), axis=1, keepdims=True)
+        coup_out[...] = total / (column + norms[1:] + EPSILON)
+        if slot is not None:
+            for some in (far_first[: group // 2], far_first[group // 2 :]):
+                @pl.when(seat < seats - 1)
+                def _():
+                    for step in some:
+                        near(above, 0, slot, step, near_up_send, near_up_recv).start()
+
+                @pl.when(seat > 0)
+                def _():
+                    for step in some:
+                        near(below, 1, slot, step, near_down_send, near_down_recv).start()
+
+        if late:
+            forward(slot, EARLY)
+        for step in far_first[:-1]:
             pltpu.make_async_remote_copy(
                 src_ref=coup_out, dst_ref=coup_in.at[step],
                 send_sem=coup_send, recv_sem=coup_recv,
                 device_id={"row": lax.rem(me + step, group)}, device_id_type=MESH,
             ).start()
+        if late:
+            for c in range(EARLY + 1, CHUNKS):
+                forward(slot, c)
         coup_in[0] = coup_out[...]
         coup_all.wait_recv()
-        coupling = jnp.concatenate(
-            [coup_in[lax.rem(me - k + group, group)] for k in range(group)], axis=0
-        )
         gram_all.wait_send()
         coup_all.wait_send()
-        return coupling
+        return assembled(coup_in)
 
     def turn(coupling, swap_rows, swap_columns):
         lead_columns, trail_columns = columns_of(coupling, coupling)
@@ -235,6 +275,99 @@
 
     def held_block(slot, c):
         return jnp.concatenate([held[slot, 0, part(c)], held[slot, 1, part(c)]], axis=1)
+
+    def forward(slot, c):
+        @pl.when(seat < seats - 1)
+        def _():
+            raw_up(slot, c).start()
+
+        @pl.when(seat > 0)
+        def _():
+            raw_down(slot, c).start()
+
+    def near_turns(now):
+        @pl.when(first)
+        def _():
+            for step in range(group):
+                coup_near[now, 0, step] = coup_in[step]
+
+        @pl.when(final)
+        def _():
+            for step in range(group):
+                coup_near[now, 1, step] = coup_in[step]
+
+        @pl.when(seat > 0)
+        def _():
+            near_all(below, 0, now, near_down_send, near_up_recv).wait_recv()
+            near_all(below, 1, now, near_down_send, near_down_recv).wait_send()
+
+        @pl.when(seat < seats - 1)
+        def _():
+            near_all(above, 1, now, near_up_send, near_down_recv).wait_recv()
+            near_all(above, 0, now, near_up_send, near_up_recv).wait_send()
+
+        low, high = assembled(coup_near.at[now, 0]), assembled(coup_near.at[now, 1])
+        (low_top, low_bottom), (high_top, high_bottom) = columns_of(
+            jnp.where(seat == 1, -low.T, low), jnp.where(final, -high.T, high)
+        )
+        lead_turn = jnp.concatenate(
+            [jnp.where(seat == 1, low_bottom, low_top), jnp.where(seat == 1, low_top, low_bottom)]
+        )
+        trail_turn = jnp.concatenate(
+            [jnp.where(final, high_bottom, high_top), jnp.where(final, high_top, high_bottom)]
+        )
+        lead_turn = jnp.concatenate(halves(lead_turn), axis=1)
+        trail_turn = jnp.concatenate(halves(trail_turn), axis=1)
+        return lead_turn, trail_turn
+
+    def near_chunk(now, c, turns):
+        lead_turn, trail_turn = turns
+
+        @pl.when(seat > 0)
+        def _():
+            raw_up(now, c).wait_recv()
+            raw_down(now, c).wait_send()
+
+        @pl.when(seat < seats - 1)
+        def _():
+            raw_down(now, c).wait_recv()
+            raw_up(now, c).wait_send()
+
+        leading = applied_half(
+            jnp.concatenate([raw[now, 0, part(c)], own[now, 1, part(c)]], axis=1), lead_turn
+        )
+        trailing = applied_half(
+            jnp.concatenate([own[now, 0, part(c)], raw[now, 1, part(c)]], axis=1), trail_turn
+        )
+        return leading, trailing
+
+    def keep_at_ends(slot, c, leading, trailing):
+        @pl.when(first)
+        def _():
+            raw[slot, 0, part(c)] = leading
+            own[slot, 1, part(c)] = trailing
+
+        @pl.when(final)
+        def _():
+            raw[slot, 1, part(c)] = trailing
+            own[slot, 0, part(c)] = leading
+
+    for c in range(AHEAD):
+        one, two = act_ref[part(c), :width], act_ref[part(c), width:]
+        leading, trailing = jnp.where(swapped, two, one), jnp.where(swapped, one, two)
+        held[1, 0, part(c)] = leading
+        held[1, 1, part(c)] = trailing
+        forward(1, c)
+
+        @pl.when(seat < seats - 1)
+        def _():
+            ahead_up(c).start()
+
+        @pl.when(seat > 0)
+        def _():
+            ahead_down(c).start()
+
+        keep_at_ends(1, c, leading, trailing)
 
     totals = None
     for c in range(CHUNKS):
@@ -245,146 +378,88 @@
         jnp.where(swapped, norm_second, norm_first),
         jnp.where(swapped, norm_first, norm_second),
     )
-    turned = turn(sum_end(), True, True)
-    for c in range(CHUNKS):
+    turned = turn(sum_end(1), True, True)
+    for c in (*range(AHEAD, CHUNKS), *range(AHEAD)):
         new = applied(act_ref[part(c)], *turned)
         own[0, 0, part(c)] = new[:, :width]
         own[0, 1, part(c)] = new[:, width:]
-
-        @pl.when(seat < seats - 1)
-        def _():
-            up_copy(c).start()
-
-        @pl.when(seat > 0)
-        def _():
-            down_copy(c).start()
-
-        @pl.when(final)
-        def _():
-            held[0, 1, part(c)] = new[:, :width]
-
-        @pl.when(first)
-        def _():
-            held[0, 0, part(c)] = new[:, width:]
-
+        if c >= AHEAD:
+            @pl.when(seat < seats - 1)
+            def _():
+                up_copy(c).start()
+
+            @pl.when(seat > 0)
+            def _():
+                down_copy(c).start()
+
+            @pl.when(final)
+            def _():
+                held[0, 1, part(c)] = new[:, :width]
+
+            @pl.when(first)
+            def _():
+                held[0, 0, part(c)] = new[:, width:]
+
+    turns = near_turns(1)
     totals = None
     for c in range(CHUNKS):
-        @pl.when(seat > 0)
-        def _():
-            up_copy(c).wait_recv()
-            down_copy(c).wait_send()
-
-        @pl.when(seat < seats - 1)
-        def _():
-            down_copy(c).wait_recv()
-            up_copy(c).wait_send()
-
-        leading, trailing = held[0, 0, part(c)], held[0, 1, part(c)]
+        if c < AHEAD:
+            @pl.when(seat > 0)
+            def _():
+                ahead_up(c).wait_recv()
+                ahead_down(c).wait_send()
+
+            @pl.when(seat < seats - 1)
+            def _():
+                ahead_down(c).wait_recv()
+                ahead_up(c).wait_send()
+
+            leading, trailing = near_chunk(1, c, turns)
+            held[0, 0, part(c)] = leading
+            held[0, 1, part(c)] = trailing
+        else:
+            @pl.when(seat > 0)
+            def _():
+                up_copy(c).wait_recv()
+                down_copy(c).wait_send()
+
+            @pl.when(seat < seats - 1)
+            def _():
+                down_copy(c).wait_recv()
+                up_copy(c).wait_send()
+
+            leading, trailing = held[0, 0, part(c)], held[0, 1, part(c)]
+        if c < EARLY:
+            forward(0, c)
         totals = gram_part(leading, trailing, totals)
-
-        @pl.when(first)
-        def _():
-            raw[0, 0, part(c)] = leading
-            own[0, 1, part(c)] = trailing
-
-        @pl.when(final)
-        def _():
-            raw[0, 1, part(c)] = trailing
-            own[0, 0, part(c)] = leading
-
-    def forward(slot, c):
-        @pl.when(seat < seats - 1)
-        def _():
-            raw_up(slot, c).start()
-
-        @pl.when(seat > 0)
-        def _():
-            raw_down(slot, c).start()
+        keep_at_ends(0, c, leading, trailing)
 
     def one_round(index, totals):
         now = lax.rem(index, 2)
         later = 1 - now
         sum_start(*totals)
 
-        @pl.when(index == 2)
-        def _():
+        @pl.when(index > 2)
+        def _():
+            turned = turn(coup_own[...], False, True)
             for c in range(CHUNKS):
-                forward(now, c)
-
-        @pl.when(index > 2)
-        def _():
-            for c in range(CHUNKS):
-                new = applied(held_block(later, c), turn_own[0], turn_own[1])
+                new = applied(held_block(later, c), *turned)
                 own[now, 0, part(c)] = jnp.where(final, held[now, 0, part(c)], new[:, :width])
                 own[now, 1, part(c)] = jnp.where(first, held[now, 1, part(c)], new[:, width:])
 
-        coupling = sum_end()
-        coup_own[now] = coupling
-
-        @pl.when(seat < seats - 1)
-        def _():
-            near_up(now).start()
-
-        @pl.when(seat > 0)
-        def _():
-            near_down(now).start()
-
-        @pl.when(first)
-        def _():
-            coup_near[now, 0] = coupling
-
-        @pl.when(final)
-        def _():
-            coup_near[now, 1] = coupling
-
-        turn_own[0], turn_own[1] = turn(coupling, False, True)
-
-        @pl.when(seat > 0)
-        def _():
-            near_up(now).wait_recv()
-            near_down(now).wait_send()
-
-        @pl.when(seat < seats - 1)
-        def _():
-            near_down(now).wait_recv()
-            near_up(now).wait_send()
-
-        low, high = coup_near[now, 0], coup_near[now, 1]
-        (low_top, low_bottom), (high_top, high_bottom) = columns_of(
-            jnp.where(seat == 1, -low.T, low), jnp.where(final, -high.T, high)
-        )
-        lead_turn = jnp.concatenate(
-            [jnp.where(seat == 1, low_bottom, low_top), jnp.where(seat == 1, low_top, low_bottom)]
-        )
-        trail_turn = jnp.concatenate(
-            [jnp.where(final, high_bottom, high_top), jnp.where(final, high_top, high_bottom)]
-        )
-        lead_turn = jnp.concatenate(halves(lead_turn), axis=1)
-        trail_turn = jnp.concatenate(halves(trail_turn), axis=1)
+        coup_own[...] = sum_end(now, True)
+
+        turns = near_turns(now)
         totals = None
         for c in range(CHUNKS):
-            @pl.when(seat > 0)
-            def _():
-                raw_up(now, c).wait_recv()
-                raw_down(now, c).wait_send()
-
-            @pl.when(seat < seats - 1)
-            def _():
-                raw_down(now, c).wait_recv()
-                raw_up(now, c).wait_send()
-
-            leading = applied_half(
-                jnp.concatenate([raw[now, 0, part(c)], own[now, 1, part(c)]], axis=1), lead_turn
-            )
-            trailing = applied_half(
-                jnp.concatenate([own[now, 0, part(c)], raw[now, 1, part(c)]], axis=1), trail_turn
-            )
+            leading, trailing = near_chunk(now, c, turns)
             held[later, 0, part(c)] = leading
             held[later, 1, part(c)] = trailing
 
-            @pl.when(index < ROUNDS - 1)
-            def _():
-                forward(later, c)
+            if c < EARLY:
+                @pl.when(index < ROUNDS - 1)
+                def _():
+                    forward(later, c)
 
             @pl.when(first)
             def _():
@@ -427,9 +502,8 @@
             pltpu.VMEM((group, band + 8, width), F32),
             pltpu.VMEM((band, width), F32),
             pltpu.VMEM((group, band, width), F32),
-            pltpu.VMEM((2, width, width), F32),
-            pltpu.VMEM((2, 2, width, width), F32),
-            pltpu.VMEM((2, columns, columns), BF16),
+            pltpu.VMEM((width, width), F32),
+            pltpu.VMEM((2, 2, group, band, width), F32),
             dma((CHUNKS,)),
             dma((CHUNKS,)),
             dma((CHUNKS,)),
@@ -438,6 +512,10 @@
             dma((2, CHUNKS)),
             dma((CHUNKS,)),
             dma((2, CHUNKS)),
+            dma((AHEAD,)),
+            dma((AHEAD,)),
+            dma((AHEAD,)),
+            dma((AHEAD,)),
             dma,
             dma((2,)),
             dma,

time: 194 us -> 167 us (0.86)
  Pallas kernels: 191 us -> 163 us
    pallas_call x1, Pallas kernels: 191 us -> 163 us  [shards(): pl.pallas_call(functools.partial(kernel, seats, group), out_shape=jax.Sha...]
where the time goes in v3:
time: 167 us
  Pallas kernels  163 us (98%)
  local copies, waits for them, and re-layouts  2.91 us (2%)
    pallas_call x1, Pallas kernels, shards(): pl.pallas_call(functools.partial(kernel, seats, group), out_shape=jax.Sha...  163 us

profile of v3, /device:TPU:31, one launch (start us, length us, event | category | flops | bytes accessed | tf_op | source)
XLA Modules:
  0.0 166.6 jit_solution(8478281108116275646)
XLA Ops:
  0.7 0.0 copy-start
  0.7 1.6 copy-done
  2.2 163.0 %shard_map.28 = f32[2048,256]{1,0:T(8,128)S(1)} custom-call(s32[1]{0:T(128)S(6)} %copy.4.lead_ref, f32[2048,256]{1,0:T(8,128)S(1)} %copy-done), custom_call_target="tpu_custom_call" | custom-call | flops 4026531840 | bytes 4194304 | tf_op jit(solution)/shard_map/pallas_call | solution.py:489
  165.3 1.3 copy.5
Async XLA Ops:
  0.7 1.6 copy-start

commit v4 on v3

--- a/solution.py
+++ b/solution.py
@@ -12,7 +12,7 @@
 STEPS = 8
 CHUNKS = 8
 EARLY = 4
-AHEAD = 3
+AHEAD = 2
 MESH = pl.DeviceIdType.MESH
 F32 = jnp.float32
 BF16 = jnp.bfloat16
@@ -82,14 +82,16 @@
 
 def kernel(
     seats, group, lead_ref, act_ref, out_ref, held, raw, own, gram_out, gram_in, coup_out, coup_in,
-    coup_own, coup_near, up_send, up_recv, down_send, down_recv, raw_up_send, raw_up_recv,
+    coup_own, coup_near, turn_own, up_send, up_recv, down_send, down_recv, raw_up_send, raw_up_recv,
     raw_down_send, raw_down_recv, ahead_up_send, ahead_up_recv, ahead_down_send, ahead_down_recv,
     near_up_send, near_up_recv, near_down_send, near_down_recv,
     gram_send, gram_recv, coup_send, coup_recv,
 ):
     rows = act_ref.shape[0]
     width = act_ref.shape[1] // 2
-    size = rows // CHUNKS
+    early_rows = rows // 2
+    sizes = [early_rows // EARLY] * EARLY + [(rows - early_rows) // (CHUNKS - EARLY)] * (CHUNKS - EARLY)
+    spans = [pl.ds(sum(sizes[:c]), sizes[c]) for c in range(CHUNKS)]
     band = width // group
     seat = lax.axis_index("pair")
     me = lax.axis_index("row")
@@ -99,24 +101,23 @@
     swapped = lead_ref[0] == 1
 
     barrier = pltpu.get_barrier_semaphore()
-    for step in range(1, group):
+    far_first = sorted(range(group), key=lambda step: abs(2 * step - group))
+    for step in far_first[:-1]:
         pl.semaphore_signal(
             barrier, inc=1, device_id={"row": lax.rem(me + step, group)}, device_id_type=MESH
         )
     for condition, other in ((seat > 0, below), (seat < seats - 1, above)):
         @pl.when(condition)
         def _():
-            for step in range(group):
+            for step in far_first:
                 pl.semaphore_signal(
                     barrier, inc=1, device_id={"pair": other, "row": lax.rem(me + step, group)},
                     device_id_type=MESH,
                 )
     beside = (seat > 0).astype(jnp.int32) + (seat < seats - 1).astype(jnp.int32)
-    pl.semaphore_wait(barrier, group - 1 + group * beside)
-    far_first = sorted(range(group), key=lambda step: abs(2 * step - group))
 
     def part(c):
-        return pl.ds(c * size, size)
+        return spans[c]
 
     def to(other, source, target, send, receive):
         return pltpu.make_async_remote_copy(
@@ -192,7 +193,7 @@
         device_id={"row": lax.rem(me + 1, group)}, device_id_type=MESH,
     )
 
-    def sum_start(cross, norm_lead, norm_trail):
+    def sum_stage(cross, norm_lead, norm_trail):
         norm_lead = jnp.sum(norm_lead, axis=0, keepdims=True)
         norm_trail = jnp.sum(norm_trail, axis=0, keepdims=True)
         line = lax.broadcasted_iota(jnp.int32, (8, width), 0)
@@ -200,6 +201,8 @@
         for k in range(group):
             gram_out[k, :band] = cross[k * band : (k + 1) * band]
             gram_out[k, band:] = norms
+
+    def sum_send():
         for step in far_first[:-1]:
             other = lax.rem(me + step, group)
             pltpu.make_async_remote_copy(
@@ -211,7 +214,7 @@
     def assembled(bands):
         return jnp.concatenate([bands[lax.rem(me - k + group, group)] for k in range(group)], axis=0)
 
-    def sum_end(slot=None, late=False):
+    def sum_end(slot=None, meanwhile=None):
         total = gram_out[me, :band]
         norms = gram_out[me, band : band + 2]
         gram_all.wait_recv()
@@ -234,7 +237,7 @@
                     for step in some:
                         near(below, 1, slot, step, near_down_send, near_down_recv).start()
 
-        if late:
+        if meanwhile is not None:
             forward(slot, EARLY)
         for step in far_first[:-1]:
             pltpu.make_async_remote_copy(
@@ -242,9 +245,10 @@
                 send_sem=coup_send, recv_sem=coup_recv,
                 device_id={"row": lax.rem(me + step, group)}, device_id_type=MESH,
             ).start()
-        if late:
+        if meanwhile is not None:
             for c in range(EARLY + 1, CHUNKS):
                 forward(slot, c)
+            meanwhile()
         coup_in[0] = coup_out[...]
         coup_all.wait_recv()
         gram_all.wait_send()
@@ -352,11 +356,25 @@
             raw[slot, 1, part(c)] = trailing
             own[slot, 0, part(c)] = leading
 
+    totals = None
+    for c in range(CHUNKS):
+        totals = gram_part(act_ref[part(c), :width], act_ref[part(c), width:], totals)
+    cross, norm_first, norm_second = totals
+    sum_stage(
+        jnp.where(swapped, cross.T, cross),
+        jnp.where(swapped, norm_second, norm_first),
+        jnp.where(swapped, norm_first, norm_second),
+    )
     for c in range(AHEAD):
         one, two = act_ref[part(c), :width], act_ref[part(c), width:]
         leading, trailing = jnp.where(swapped, two, one), jnp.where(swapped, one, two)
         held[1, 0, part(c)] = leading
         held[1, 1, part(c)] = trailing
+        keep_at_ends(1, c, leading, trailing)
+
+    pl.semaphore_wait(barrier, group - 1 + group * beside)
+    sum_send()
+    for c in range(AHEAD):
         forward(1, c)
 
         @pl.when(seat < seats - 1)
@@ -367,17 +385,6 @@
         def _():
             ahead_down(c).start()
 
-        keep_at_ends(1, c, leading, trailing)
-
-    totals = None
-    for c in range(CHUNKS):
-        totals = gram_part(act_ref[part(c), :width], act_ref[part(c), width:], totals)
-    cross, norm_first, norm_second = totals
-    sum_start(
-        jnp.where(swapped, cross.T, cross),
-        jnp.where(swapped, norm_second, norm_first),
-        jnp.where(swapped, norm_first, norm_second),
-    )
     turned = turn(sum_end(1), True, True)
     for c in (*range(AHEAD, CHUNKS), *range(AHEAD)):
         new = applied(act_ref[part(c)], *turned)
@@ -437,17 +444,22 @@
     def one_round(index, totals):
         now = lax.rem(index, 2)
         later = 1 - now
-        sum_start(*totals)
+        sum_stage(*totals)
+        sum_send()
 
         @pl.when(index > 2)
         def _():
-            turned = turn(coup_own[...], False, True)
-            for c in range(CHUNKS):
-                new = applied(held_block(later, c), *turned)
-                own[now, 0, part(c)] = jnp.where(final, held[now, 0, part(c)], new[:, :width])
-                own[now, 1, part(c)] = jnp.where(first, held[now, 1, part(c)], new[:, width:])
-
-        coup_own[...] = sum_end(now, True)
+            turn_own[0], turn_own[1] = turn(coup_own[...], False, True)
+
+        def own_blocks():
+            @pl.when(index > 2)
+            def _():
+                for c in range(CHUNKS):
+                    new = applied(held_block(later, c), turn_own[0], turn_own[1])
+                    own[now, 0, part(c)] = jnp.where(final, held[now, 0, part(c)], new[:, :width])
+                    own[now, 1, part(c)] = jnp.where(first, held[now, 1, part(c)], new[:, width:])
+
+        coup_own[...] = sum_end(now, own_blocks)
 
         turns = near_turns(now)
         totals = None
@@ -474,7 +486,8 @@
 
     totals = lax.fori_loop(2, ROUNDS, one_round, totals)
     last = ROUNDS % 2
-    sum_start(*totals)
+    sum_stage(*totals)
+    sum_send()
     turned = turn(sum_end(), False, False)
     for c in range(CHUNKS):
         out_ref[part(c)] = applied(held_block(last, c), *turned)
@@ -504,6 +517,7 @@
             pltpu.VMEM((group, band, width), F32),
             pltpu.VMEM((width, width), F32),
             pltpu.VMEM((2, 2, group, band, width), F32),
+            pltpu.VMEM((2, columns, columns), BF16),
             dma((CHUNKS,)),
             dma((CHUNKS,)),
             dma((CHUNKS,)),

time: 167 us -> 166 us (level)
  no operation moved by 1% of the time
where the time goes in v4:
time: 166 us; the launch traced here: 165 us
  Pallas kernels  162 us (98%)
  local copies, waits for them, and re-layouts  2.91 us (2%)
    pallas_call x1, Pallas kernels, shards(): pl.pallas_call(functools.partial(kernel, seats, group), out_shape=jax.Sha...  162 us

profile of v4, /device:TPU:31, one launch (start us, length us, event | category | flops | bytes accessed | tf_op | source)
XLA Modules:
  0.0 165.5 jit_solution(4831356417152355176)
XLA Ops:
  0.7 0.0 copy-start
  0.7 1.6 copy-done
  2.2 161.9 %shard_map.28 = f32[2048,256]{1,0:T(8,128)S(1)} custom-call(s32[1]{0:T(128)S(6)} %copy.4.lead_ref, f32[2048,256]{1,0:T(8,128)S(1)} %copy-done), custom_call_target="tpu_custom_call" | custom-call | flops 4026531840 | bytes 4194304 | tf_op jit(solution)/shard_map/pallas_call | solution.py:502
  164.1 1.3 copy.5
Async XLA Ops:
  0.7 1.6 copy-start

commit v5 on v4

--- a/solution.py
+++ b/solution.py
@@ -84,7 +84,7 @@
     seats, group, lead_ref, act_ref, out_ref, held, raw, own, gram_out, gram_in, coup_out, coup_in,
     coup_own, coup_near, turn_own, up_send, up_recv, down_send, down_recv, raw_up_send, raw_up_recv,
     raw_down_send, raw_down_recv, ahead_up_send, ahead_up_recv, ahead_down_send, ahead_down_recv,
-    near_up_send, near_up_recv, near_down_send, near_down_recv,
+    relay_send, relay_recv, near_up_send, near_up_recv, near_down_send, near_down_recv,
     gram_send, gram_recv, coup_send, coup_recv,
 ):
     rows = act_ref.shape[0]
@@ -158,13 +158,30 @@
 
     def near(other, side, slot, step, send, receive):
         return pltpu.make_async_remote_copy(
-            src_ref=coup_out, dst_ref=coup_near.at[slot, side, step],
+            src_ref=coup_out, dst_ref=coup_near.at[slot, side, 0, step // 2],
             send_sem=send, recv_sem=receive.at[slot],
             device_id={"pair": other, "row": lax.rem(me + step, group)}, device_id_type=MESH,
         )
 
     def near_all(other, side, slot, send, receive):
-        return to(other, coup_near.at[slot, side], coup_near.at[slot, side], send, receive.at[slot])
+        bands = coup_near.at[slot, side, 0]
+        return to(other, bands, bands, send, receive.at[slot])
+
+    mate = me + 1 - 2 * lax.rem(me, 2)
+
+    def relay(slot, side):
+        return pltpu.make_async_remote_copy(
+            src_ref=coup_near.at[slot, side, 0], dst_ref=coup_near.at[slot, side, 1],
+            send_sem=relay_send.at[side], recv_sem=relay_recv.at[slot, side],
+            device_id={"row": mate}, device_id_type=MESH,
+        )
+
+    def near_assembled(slot, side):
+        rows_of = []
+        for k in range(group):
+            lane = lax.rem(me // 2 - k // 2 + group // 2, group // 2)
+            rows_of.append(coup_near[slot, side, lax.rem(me + k, 2), lane])
+        return jnp.concatenate(rows_of, axis=0)
 
     def gram_part(leading, trailing, totals):
         lead_high, lead_low = halves(leading)
@@ -226,7 +243,8 @@
         column = jnp.sum(jnp.where(mine, norms[:1], 0.0), axis=1, keepdims=True)
         coup_out[...] = total / (column + norms[1:] + EPSILON)
         if slot is not None:
-            for some in (far_first[: group // 2], far_first[group // 2 :]):
+            even = [step for step in far_first if step % 2 == 0]
+            for some in (even[: group // 4], even[group // 4 :]):
                 @pl.when(seat < seats - 1)
                 def _():
                     for step in some:
@@ -292,25 +310,39 @@
     def near_turns(now):
         @pl.when(first)
         def _():
-            for step in range(group):
-                coup_near[now, 0, step] = coup_in[step]
+            for lane in range(group // 2):
+                coup_near[now, 0, 0, lane] = coup_in[2 * lane]
+                other = lax.rem(me - mate + 2 * lane + group, group)
+                coup_near[now, 0, 1, lane] = coup_in[other]
 
         @pl.when(final)
         def _():
-            for step in range(group):
-                coup_near[now, 1, step] = coup_in[step]
+            for lane in range(group // 2):
+                coup_near[now, 1, 0, lane] = coup_in[2 * lane]
+                other = lax.rem(me - mate + 2 * lane + group, group)
+                coup_near[now, 1, 1, lane] = coup_in[other]
 
         @pl.when(seat > 0)
         def _():
             near_all(below, 0, now, near_down_send, near_up_recv).wait_recv()
+            relay(now, 0).start()
+
+        @pl.when(seat < seats - 1)
+        def _():
+            near_all(above, 1, now, near_up_send, near_down_recv).wait_recv()
+            relay(now, 1).start()
+
+        @pl.when(seat > 0)
+        def _():
             near_all(below, 1, now, near_down_send, near_down_recv).wait_send()
+            relay(now, 0).wait()
 
         @pl.when(seat < seats - 1)
         def _():
-            near_all(above, 1, now, near_up_send, near_down_recv).wait_recv()
             near_all(above, 0, now, near_up_send, near_up_recv).wait_send()
-
-        low, high = assembled(coup_near.at[now, 0]), assembled(coup_near.at[now, 1])
+            relay(now, 1).wait()
+
+        low, high = near_assembled(now, 0), near_assembled(now, 1)
         (low_top, low_bottom), (high_top, high_bottom) = columns_of(
             jnp.where(seat == 1, -low.T, low), jnp.where(final, -high.T, high)
         )
@@ -516,7 +548,7 @@
             pltpu.VMEM((band, width), F32),
             pltpu.VMEM((group, band, width), F32),
             pltpu.VMEM((width, width), F32),
-            pltpu.VMEM((2, 2, group, band, width), F32),
+            pltpu.VMEM((2, 2, 2, group // 2, band, width), F32),
             pltpu.VMEM((2, columns, columns), BF16),
             dma((CHUNKS,)),
             dma((CHUNKS,)),
@@ -530,6 +562,8 @@
             dma((AHEAD,)),
             dma((AHEAD,)),
             dma((AHEAD,)),
+            dma((2,)),
+            dma((2, 2)),
             dma,
             dma((2,)),
             dma,

time: 166 us -> 161 us (0.970)
  Pallas kernels: 162 us -> 157 us
    pallas_call x1, Pallas kernels: 162 us -> 157 us  [shards(): pl.pallas_call(functools.partial(kernel, seats, group), out_shape=jax.Sha...]
where the time goes in v5:
time: 161 us; the launch traced here: 160 us
  Pallas kernels  157 us (98%)
  local copies, waits for them, and re-layouts  2.91 us (2%)
    pallas_call x1, Pallas kernels, shards(): pl.pallas_call(functools.partial(kernel, seats, group), out_shape=jax.Sha...  157 us

profile of v5, /device:TPU:31, one launch (start us, length us, event | category | flops | bytes accessed | tf_op | source)
XLA Modules:
  0.0 160.4 jit_solution(14906189114708998748)
XLA Ops:
  0.7 0.0 copy-start
  0.7 1.6 copy-done
  2.2 156.8 %shard_map.28 = f32[2048,256]{1,0:T(8,128)S(1)} custom-call(s32[1]{0:T(128)S(6)} %copy.4.lead_ref, f32[2048,256]{1,0:T(8,128)S(1)} %copy-done), custom_call_target="tpu_custom_call" | custom-call | flops 4026531840 | bytes 4194304 | tf_op jit(solution)/shard_map/pallas_call | solution.py:534
  159.1 1.3 copy.5
Async XLA Ops:
  0.7 1.6 copy-start
